TPU v7x, 32 devices: a whole 2x2x4 slice. The times are simulated.
32 devices in a mesh: wide: 8 (over z, x), narrow: 4 (over y, core).
Axes of the slice: x: 2, y: 2, z: 4, core: 2. Of those that a mesh axis runs over, the one named last changes fastest.
Arguments:
- tensor: bfloat16 [32, 3, 1024, 1024], P('wide', None, 'narrow'), may hold values from -6 to 6
- occupied: bfloat16 [32, 3, 1024], replicated, may hold values from -0.625 to 0.625
- virtual: bfloat16 [32, 3, 1024], replicated, may hold values from -0.001953125 to 0.001953125
- atom_size: int32 [32], replicated, may hold values from 14 to 32, as said below
- tensor_pattern: int32 [32, 3], replicated, may hold values 0 or 1
- occupied_pattern: int32 [32, 3], replicated, may hold values 0 or 1
- virtual_pattern: int32 [32, 3], replicated, may hold values 0 or 1
Outputs:
- response: float32 [1024, 1024], P('wide', 'narrow')
Inputs may be any that keep to these rules, and one draw needn't show every extreme that they name: Orbitals of an atom at and beyond its atom_size are padding.
All inputs are finite; a program needn't handle non-finite values.
Results may differ from a plain program's by a relative error of at most 0.0041.
Values may be sent and summed in bfloat16 or wider, within the bound.
A program may use at most 192 MiB of HBM per device.

v0:
```python
import jax
import jax.numpy as jnp
from jax import lax
from jax.sharding import PartitionSpec as P

BO = 32


def with_halo(array, sides, width):
    for axis, dim in sides:
        devices, length = (lax.axis_size(axis), array.shape[dim])
        up = [(i, (i + 1) % devices) for i in range(devices - 1)]
        down = [(j, i) for i, j in up]
        last = lax.slice_in_dim(array, length - width, length, axis=dim)
        initial = lax.slice_in_dim(array, 0, width, axis=dim)
        before = lax.ppermute(last, axis, up)
        after = lax.ppermute(initial, axis, down)
        array = jnp.concatenate([before, array, after], axis=dim)
    return array


def block_masks(size_pad, tensor_flags, occupied_flags, virtual_flags, atom_index):
    nearby_sizes = lax.dynamic_slice(size_pad, (atom_index,), (5,))
    present = (nearby_sizes > 0).astype(jnp.int32)
    orbital = jnp.arange(BO, dtype=jnp.int32)
    zero_index = jnp.zeros((), jnp.int32)
    row_flags = lax.dynamic_slice(tensor_flags, (atom_index + 1, zero_index), (3, 3))
    row_ok = (orbital[None, :] < nearby_sizes[1:4, None]).astype(jnp.int32)
    partner = jnp.stack([nearby_sizes[r : r + 3] for r in range(3)])
    column_ok = (orbital[None, None, :] < partner[:, :, None]).astype(jnp.int32)
    entry_mask = row_flags[:, :, None, None] * row_ok[:, None, :, None] * column_ok[:, :, None, :]
    tensor_mask = entry_mask.reshape(3, 3, 1, BO * BO).astype(jnp.bfloat16)
    occupied_mask = (
        lax.dynamic_slice(occupied_flags, (atom_index + 2, zero_index), (1, 3))[0] * present[1:4]
    )
    partner_present = jnp.stack([present[r : r + 3] for r in range(3)])
    virtual_mask = (
        lax.dynamic_slice(virtual_flags, (atom_index + 1, zero_index), (3, 3))
        * present[1:4, None]
        * partner_present
    )
    return (tensor_mask, occupied_mask.astype(jnp.bfloat16), virtual_mask.astype(jnp.bfloat16))


def contract(row_blocks, occupied_row, virtual_rows):
    ri_count = row_blocks.shape[2]
    blocks = row_blocks.reshape(3, 3, ri_count, BO, BO)
    occupied_blocks = occupied_row.reshape(3, BO, BO)
    virtual_blocks = virtual_rows.reshape(3, 3, BO, BO)
    occupied_terms = []
    virtual_terms = []
    for out_band in range(5):
        total_left = jnp.zeros((ri_count, BO, BO), jnp.float32)
        total_right = jnp.zeros((ri_count, BO, BO), jnp.float32)
        for left_band in range(3):
            right_band = out_band - left_band
            if 0 <= right_band < 3:
                total_left = total_left + jnp.einsum(
                    "lm,pmn->pln",
                    occupied_blocks[left_band],
                    blocks[left_band, right_band],
                    preferred_element_type=jnp.float32,
                )
                total_right = total_right + jnp.einsum(
                    "pls,sn->pln",
                    blocks[1, left_band],
                    virtual_blocks[left_band, right_band],
                    preferred_element_type=jnp.float32,
                )
        occupied_terms.append(total_left.reshape(ri_count, BO * BO))
        virtual_terms.append(total_right.reshape(ri_count, BO * BO))
    left_product = jnp.stack(occupied_terms, 1).reshape(ri_count, 5 * BO * BO).astype(jnp.bfloat16)
    right_product = jnp.stack(virtual_terms, 1).reshape(ri_count, 5 * BO * BO).astype(jnp.bfloat16)
    return (left_product, right_product)


def body(tensor, occupied, virtual, atom_size, tensor_pattern, occupied_pattern, virtual_pattern):
    narrow_count = lax.axis_size("narrow")
    atom_index = lax.axis_index("wide") * narrow_count + lax.axis_index("narrow")
    sectioned_rows = tensor[:, None]
    regrouped = lax.all_to_all(sectioned_rows, "narrow", split_axis=0, concat_axis=3, tiled=True)
    row_blocks = with_halo(regrouped[:, 0], ((("wide", "narrow"), 0),), 1)
    occupied_pad = jnp.pad(occupied, ((1, 1), (0, 0), (0, 0)))
    virtual_pad = jnp.pad(virtual, ((1, 1), (0, 0), (0, 0)))
    size_pad = jnp.pad(atom_size, 2)
    tensor_flags = jnp.pad(tensor_pattern, ((2, 2), (0, 0)))
    occupied_flags = jnp.pad(occupied_pattern, ((2, 2), (0, 0)))
    virtual_flags = jnp.pad(virtual_pattern, ((2, 2), (0, 0)))
    tensor_mask, occupied_mask, virtual_mask = block_masks(
        size_pad, tensor_flags, occupied_flags, virtual_flags, atom_index
    )
    row_blocks = row_blocks * tensor_mask
    occupied_row = (
        lax.dynamic_slice_in_dim(occupied_pad, atom_index + 1, 1, 0)[0] * occupied_mask[:, None]
    )
    virtual_rows = (
        lax.dynamic_slice_in_dim(virtual_pad, atom_index, 3, 0) * virtual_mask[:, :, None]
    )
    left_product, right_product = contract(row_blocks, occupied_row, virtual_rows)
    partial_response = lax.dot_general(
        left_product, right_product, (((1,), (1,)), ((), ())), preferred_element_type=jnp.float32
    )
    column_share = lax.psum_scatter(partial_response, "narrow", scatter_dimension=1, tiled=True)
    response = lax.psum_scatter(column_share, "wide", scatter_dimension=0, tiled=True)
    return response


def solution(mesh):
    placed = (P("wide", None, "narrow", None), P(), P(), P(), P(), P(), P())
    return jax.shard_map(
        body, mesh=mesh, in_specs=placed, out_specs=P("wide", "narrow"), check_vma=False
    )
```

profile of v0, /device:TPU:0, one launch (start us, length us, event | category | flops | bytes accessed | tf_op | source)
XLA Modules:
  0.0 552.6 jit_solution(14815793715952923454)
XLA Ops:
  6.5 75.2 %all_to_all.15 = bf16[4,1,3,256,1024]{4,3,2,1,0:T(8,128)(2,1)S(1)} all-to-all(bf16[4,1,3,256,1024]{4,3,2,1,0:T(8,128)(2,1)} %bitcast.164), channel_id=1, replica_groups=mesh['wide'=8,'narrow'=4] {'narrow'}, dimensions={0} | all-to-all | bytes 12582912 | tf_op jit(solution)/shard_map/all_to_all | solution.py:81
  86.5 5.7 %collective-permute-start = (bf16[1,3,1024,1024]{3,2,1,0:T(8,128)(2,1)}, bf16[1,3,1024,1024]{3,2,1,0:T(8,128)(2,1)}, u32[]{:S(2)}, u32[]{:S(2)}) collective-permute-start(bf16[1,3,1024,1024]{3,2,1,0:T(8,128)(2,1)} %bitcast.3), channel_id=1, source_target_pairs={{0,1},{1,2},{2,3},{3,4},{4,5},{5,6},{6,7},{7,8},{8,9},{9,10},{10,1... | collective-permute-start | bytes 18874376 | tf_op jit(solution)/shard_map/ppermute | solution.py:16
  93.9 10.6 %copy.71 = bf16[1,1,3,4,256,1024]{4,3,5,2,1,0:T(4,128)(2,1)} copy(bf16[1,1,3,4,256,1024]{5,4,3,2,1,0:T(8,128)(2,1)} %bitcast.149) | data formatting | bytes 12582912 | tf_op jit(solution)/shard_map/all_to_all | solution.py:81
  104.5 11.0 %concatenate.11 = bf16[1,3,1024,32,32]{2,4,3,1,0:T(8,128)(2,1)} reshape(bf16[1,1,3,4,256,1024]{4,3,5,2,1,0:T(4,128)(2,1)} %copy.71) | data formatting | bytes 12582912 | tf_op jit(solution)/shard_map/concatenate | solution.py:18
  115.5 8.9 %copy.74 = bf16[1,3,1024,32,32]{2,3,4,1,0:T(8,128)(2,1)} copy(bf16[1,3,1024,32,32]{2,4,3,1,0:T(8,128)(2,1)} %concatenate.11) | data formatting | bytes 12582912 | tf_op jit(solution)/shard_map/concatenate | solution.py:18
  124.4 8.6 %copy.72 = bf16[1,3,1024,1024]{2,3,1,0:T(8,128)(2,1)} copy(bf16[1,3,1024,1024]{3,2,1,0:T(8,128)(2,1)} %collective-permute-done.1) | data formatting | bytes 12582912 | tf_op jit(solution)/shard_map/ppermute | solution.py:17
  133.0 8.9 %copy.75 = bf16[1,3,1024,32,32]{2,3,4,1,0:T(8,128)(2,1)} copy(bf16[1,3,1024,32,32]{2,4,3,1,0:T(8,128)(2,1)} %bitcast.150) | data formatting | bytes 12582912 | tf_op jit(solution)/shard_map/concatenate | solution.py:18
  141.9 8.9 %copy.70 = bf16[1,3,1024,1024]{2,3,1,0:T(8,128)(2,1)} copy(bf16[1,3,1024,1024]{3,2,1,0:T(8,128)(2,1)} %collective-permute-done) | data formatting | bytes 12582912 | tf_op jit(solution)/shard_map/ppermute | solution.py:16
  150.9 9.1 %copy.73 = bf16[1,3,1024,32,32]{2,3,4,1,0:T(8,128)(2,1)} copy(bf16[1,3,1024,32,32]{2,4,3,1,0:T(8,128)(2,1)} %bitcast.151) | data formatting | bytes 12582912 | tf_op jit(solution)/shard_map/concatenate | solution.py:18
  160.0 8.5 %maximum_multiply_fusion = bf16[3,3,1024,32,32]{2,3,4,1,0:T(8,128)(2,1)S(1)} fusion(bf16[1,3,1024,32,32]{2,3,4,1,0:T(8,128)(2,1)} %copy.75, bf16[1,3,1024,32,32]{2,3,4,1,0:T(8,128)(2,1)S(1)} %bitcast.153, bf16[1,3,1024,32,32]{2,3,4,1,0:T(8,128)(2,1)} %copy.73, bf16[3,3,32,32]{2,3,1,0:T(8,128)(2,1)S(1)} %multiply_convert_fusion), kind=kLoop, calls=%fused_computation | loop fusion | flops 28311552 | bytes 37767168 | tf_op jit(solution)/shard_map/mul | solution.py:92
  185.8 4.9 fusion.13
  190.8 5.0 fusion.11
  195.8 4.3 convolution_convert_fusion.1
  200.1 5.2 fusion.18
  205.3 5.0 fusion.16
  245.4 4.8 fusion.5
  256.6 5.9 %convolution_convert_fusion = bf16[1024,32,32]{0,2,1:T(8,128)(2,1)} fusion(bf16[1024,32,32]{0,1,2:T(8,128)(2,1)} %get-tuple-element.10, bf16[3,3,32,32]{3,2,0,1:T(8,128)(2,1)S(1)} %reshape.88), kind=kOutput, calls=%fused_computation.23 | convolution fusion | flops 68157440 | bytes 4202496 | tf_op jit(solution)/shard_map/pls,sn->pln/dot_general | solution.py:64
  270.4 7.1 %add_convert_fusion = bf16[1024,32,32]{0,2,1:T(8,128)(2,1)} fusion(f32[1024,32,32]{0,2,1:T(8,128)} %fusion.13, bf16[1024,32,32]{0,1,2:T(8,128)(2,1)} %get-tuple-element.10, bf16[3,3,32,32]{3,2,0,1:T(8,128)(2,1)S(1)} %reshape.88), kind=kOutput, calls=%fused_computation.1 | convolution fusion | flops 69206016 | bytes 8396800 | tf_op jit(solution)/shard_map/pls,sn->pln/dot_general | solution.py:64
  277.5 4.2 copy.111
  281.7 8.5 %add_convert_fusion.1 = bf16[1024,32,32]{0,2,1:T(8,128)(2,1)} fusion(f32[1024,32,32]{0,2,1:T(8,128)} %fusion.18, f32[1024,32,32]{0,2,1:T(8,128)} %fusion.11, bf16[1024,32,32]{0,1,2:T(8,128)(2,1)} %get-tuple-element.10, bf16[3,3,32,32]{3,2,0,1:T(8,128)(2,1)S(1)} %reshape.88), kind=kOutput, calls=%fused_computation.2 | convolution fusion | flops 70254592 | bytes 12591104 | tf_op jit(solution)/shard_map/pls,sn->pln/dot_general | solution.py:64
  294.1 6.4 %add_convert_fusion.2 = bf16[1024,32,32]{0,2,1:T(8,128)(2,1)} fusion(f32[1024,32,32]{0,2,1:T(8,128)} %fusion.16, bf16[1024,32,32]{0,1,2:T(8,128)(2,1)S(1)} %get-tuple-element.11, bf16[3,3,32,32]{3,2,0,1:T(8,128)(2,1)S(1)} %reshape.88), kind=kOutput, calls=%fused_computation.3 | convolution fusion | flops 69206016 | bytes 8396800 | tf_op jit(solution)/shard_map/pls,sn->pln/dot_general | solution.py:64
  316.2 15.4 %convolution_bitcast_fusion = f32[1024,1024]{1,0:T(8,128)} fusion(bf16[1024,5,1024]{2,0,1:T(8,128)(2,1)S(1)} %constant_dynamic-update-slice_fusion, bf16[1024,5,1024]{2,0,1:T(8,128)(2,1)} %copy-done.10), kind=kOutput, calls=%fused_computation.7 | convolution fusion | flops 10737418240 | bytes 25165824 | tf_op jit(solution)/shard_map/dot_general | solution.py:100
  331.6 145.7 %reduce-scatter.3.cloned.1.call-done = f32[1024,256]{1,0:T(8,128)} async-done(((f32[1024,1024]{1,0:T(8,128)}), f32[1024,256]{1,0:T(8,128)}) %reduce-scatter.3.cloned.1.call-update) | async-done | bytes 1048592 | tf_op jit(solution)/shard_map/reduce_scatter | solution.py:103
  477.3 67.9 %reduce-scatter.5.cloned.1.call-done = f32[128,256]{1,0:T(8,128)} async-done(((f32[1024,256]{1,0:T(8,128)}), f32[128,256]{1,0:T(8,128)}) %reduce-scatter.5.cloned.1.call-update) | async-done | bytes 131088 | tf_op jit(solution)/shard_map/reduce_scatter | solution.py:104
  (101 shorter events, 92.6 us)
Async XLA Ops:
  6.5 470.8 %reduce-scatter.3.cloned.1.call-start = ((), (), s32[]{:S(2)}) async-start(), calls=%async_computation.3 | async-start | bytes 5242880 | tf_op jit(solution)/shard_map/reduce_scatter | solution.py:103
  81.8 10.4 %copy-start.15 = (s32[32,3]{0,1:T(4,128)S(1)}, s32[32,3]{0,1:T(4,128)}, u32[]{:S(2)}) copy-start(s32[32,3]{0,1:T(4,128)} %param.11) | copy-start | bytes 1156
  81.8 10.6 %copy-start.14 = (s32[32,3]{0,1:T(4,128)S(1)}, s32[32,3]{0,1:T(4,128)}, u32[]{:S(2)}) copy-start(s32[32,3]{0,1:T(4,128)} %param.12) | copy-start | bytes 1156
  81.8 10.8 %copy-start.16 = (s32[32]{0:T(128)S(1)}, s32[32]{0:T(128)}, u32[]{:S(2)}) copy-start(s32[32]{0:T(128)} %param.10) | copy-start | bytes 388
  81.8 10.8 %copy-start.11 = (bf16[32,3,1024]{2,0,1:T(8,128)(2,1)S(1)}, bf16[32,3,1024]{2,0,1:T(8,128)(2,1)}, u32[]{:S(2)}) copy-start(bf16[32,3,1024]{2,0,1:T(8,128)(2,1)} %param.8) | copy-start | bytes 589828
  81.8 11.3 %copy-start.13 = (s32[32,3]{0,1:T(4,128)S(1)}, s32[32,3]{0,1:T(4,128)}, u32[]{:S(2)}) copy-start(s32[32,3]{0,1:T(4,128)} %param.13) | copy-start | bytes 1156
  81.8 11.6 %copy-start.12 = (bf16[32,3,1024]{2,0,1:T(8,128)(2,1)S(1)}, bf16[32,3,1024]{2,0,1:T(8,128)(2,1)}, u32[]{:S(2)}) copy-start(bf16[32,3,1024]{2,0,1:T(8,128)(2,1)} %param.9) | copy-start | bytes 589828
  85.2 39.2 %collective-permute-start.1 = (bf16[1,3,1024,1024]{3,2,1,0:T(8,128)(2,1)}, bf16[1,3,1024,1024]{3,2,1,0:T(8,128)(2,1)}, u32[]{:S(2)}, u32[]{:S(2)}) collective-permute-start(bf16[1,3,1024,1024]{3,2,1,0:T(8,128)(2,1)} %bitcast.3), channel_id=1, source_target_pairs={{1,0},{2,1},{3,2},{4,3},{5,4},{6,5},{7,6},{8,7},{9,8},{10,9},{11,1... | collective-permute-start | bytes 18874376 | tf_op jit(solution)/shard_map/ppermute | solution.py:17
  86.5 55.4 %collective-permute-start = (bf16[1,3,1024,1024]{3,2,1,0:T(8,128)(2,1)}, bf16[1,3,1024,1024]{3,2,1,0:T(8,128)(2,1)}, u32[]{:S(2)}, u32[]{:S(2)}) collective-permute-start(bf16[1,3,1024,1024]{3,2,1,0:T(8,128)(2,1)} %bitcast.3), channel_id=1, source_target_pairs={{0,1},{1,2},{2,3},{3,4},{4,5},{5,6},{6,7},{7,8},{8,9},{9,10},{10,1... | collective-permute-start | bytes 18874376 | tf_op jit(solution)/shard_map/ppermute | solution.py:16
  150.9 9.1 %slice-start = ((s8[6291456]{0:T(1024)(128)(4,1)}), s8[4194304]{0:T(1024)(128)(4,1)S(1)}, s32[]{:S(2)}) async-start(s8[6291456]{0:T(1024)(128)(4,1)} %bitcast.152), calls=%async_computation.5 | async-start | bytes 8388608
  150.9 9.1 %slice-start.1 = ((s8[6291456]{0:T(1024)(128)(4,1)}), s8[2097152]{0:T(1024)(128)(4,1)S(1)}, s32[]{:S(2)}) async-start(s8[6291456]{0:T(1024)(128)(4,1)} %bitcast.152), calls=%async_computation.6 | async-start | bytes 4194304
  168.5 41.8 %copy-start = (bf16[3,3,1024,32,32]{2,3,4,1,0:T(8,128)(2,1)}, bf16[3,3,1024,32,32]{2,3,4,1,0:T(8,128)(2,1)S(1)}, u32[]{:S(2)}) copy-start(bf16[3,3,1024,32,32]{2,3,4,1,0:T(8,128)(2,1)S(1)} %maximum_multiply_fusion) | copy-start | bytes 56623108
  300.6 6.0 %copy-start.4 = (bf16[1024,1,1024]{2,0,1:T(8,128)(2,1)S(1)}, bf16[1024,1,1024]{2,0,1:T(8,128)(2,1)}, u32[]{:S(2)}) copy-start(bf16[1024,1,1024]{2,0,1:T(8,128)(2,1)} %copy.82) | copy-start | bytes 6291460
  304.7 2.2 copy-start.9
  306.6 1.7 copy-start.8
  306.9 2.0 copy-start.7
  308.2 1.7 copy-start.6
  308.9 1.7 copy-start.3
  310.0 1.8 copy-start.5
  310.6 5.0 copy-start.10
  310.6 3.4 copy-start.2
  311.8 4.3 copy-start.1
  331.6 213.7 %reduce-scatter.5.cloned.1.call-start = ((), (), s32[]{:S(2)}) async-start(), calls=%async_computation.4 | async-start | bytes 1179648 | tf_op jit(solution)/shard_map/reduce_scatter | solution.py:104
Sparse Core Ops, SparseCore 0:
  331.7 145.5 reduce-scatter.2
  481.1 64.1 reduce-scatter.4
where the time goes:
time: 562 us; the launch traced here: 553 us
  waiting for transfers between devices  214 us (38%)
  local copies, waits for them, and re-layouts  138 us (25%)
  matrix products  95.1 us (17%)
  blocking collectives  75.2 us (13%)
  between operations  14.1 us (3%)
  other arithmetic  9.27 us (2%)
  starting transfers between devices  7.01 us (1%)
    reduce_scatter x1, waiting for transfers between devices, body(): lax.psum_scatter(partial_response, 'narrow', scatter_dimension=1, tiled=T...  146 us
    all_to_all x1, blocking collectives, body(): lax.all_to_all(sectioned_rows, 'narrow', split_axis=0, concat_axis=3, til...  75.2 us
    reduce_scatter x1, waiting for transfers between devices, body(): lax.psum_scatter(column_share, 'wide', scatter_dimension=0, tiled=True)  67.9 us
    dot_general x9, matrix products, contract(): jnp.einsum('pls,sn->pln', blocks[1, left_band], virtual_blocks[left_band,...  52.4 us
    concatenate x4, local copies, waits for them, and re-layouts, with_halo(): array = jnp.concatenate([before, array, after], axis=dim)  37.9 us
    dot_general x9, matrix products, contract(): jnp.einsum('lm,pmn->pln', occupied_blocks[left_band], blocks[left_band, r...  27.3 us
    another operation x6, local copies, waits for them, and re-layouts, contract(): jnp.stack(virtual_terms, 1).reshape(ri_count, 5 * BO * BO)  20.2 us
    another operation x6, local copies, waits for them, and re-layouts, contract(): jnp.stack(occupied_terms, 1).reshape(ri_count, 5 * BO * BO)  20 us
  transfers between devices with their start and end apart: 4, of which 2 were waited for; matrix products, arithmetic and copies ran while one was open for 9% of the time, Pallas kernels for 0%

commit v1 on v0

v1 whole, which is shorter than its diff:
```python
import jax
import jax.numpy as jnp
from jax import lax
from jax.experimental import pallas as pl
from jax.experimental.pallas import tpu as pltpu
from jax.sharding import PartitionSpec as P

BO = 32
LANES = BO * BO
GROUP = 256
VMEM_LIMIT = 56 * 1024 * 1024


def weight_kernel(before, here, after, mask, kron_v, occ_cols, delta, out, kron_o, right, total):
    i = pl.program_id(0)
    ri = here.shape[2]
    for co, rows in enumerate((before, here, after)):
        for lam in range(BO):
            kron_o[lam * BO : (lam + 1) * BO, :] = occ_cols[0, co, lam : lam + 1, :] * delta[...]
        blocks = [rows[0, ds] * mask[i + co, ds : ds + 1, :] for ds in range(3)]
        for bo in range(3):
            for g in range(LANES // GROUP):
                lanes = slice(g * GROUP, (g + 1) * GROUP)
                acc = None
                for ds in range(3):
                    e = bo + 2 - (co + ds)
                    if 0 <= e < 3:
                        term = jnp.dot(
                            blocks[ds][:, lanes],
                            kron_v[i + co + ds, e],
                            preferred_element_type=jnp.float32,
                        )
                        acc = term if acc is None else acc + term
                right[bo * ri : (bo + 1) * ri, lanes] = acc.astype(jnp.bfloat16)
        product = jnp.dot(right[...], kron_o[...], preferred_element_type=jnp.float32)
        if co == 0:
            total[...] = product
        elif co == 1:
            total[...] += product
        else:
            for bo in range(3):
                rows_of = slice(bo * ri, (bo + 1) * ri)
                value = total[rows_of, :] + product[rows_of, :]
                keep = mask[i + 1, bo : bo + 1, :].astype(jnp.float32)
                out[0, bo] = (value * keep).astype(jnp.bfloat16)


def weights(rows, mask, kron_v, occ_cols, delta):
    atoms = rows.shape[0] - 2
    ri = rows.shape[2]
    row_spec = lambda shift: pl.BlockSpec((1, 3, ri, LANES), lambda i, s=shift: (i + s, 0, 0, 0))
    full = lambda a: pl.BlockSpec(a.shape, lambda i, r=a.ndim: (0,) * r)
    flops = atoms * 2 * ri * LANES * (19 * GROUP + 9 * LANES)
    return pl.pallas_call(
        weight_kernel,
        grid=(atoms,),
        out_shape=jax.ShapeDtypeStruct((atoms, 3, ri, LANES), jnp.bfloat16),
        in_specs=[
            row_spec(0),
            row_spec(1),
            row_spec(2),
            full(mask),
            full(kron_v),
            pl.BlockSpec((1, 3, BO, LANES), lambda i: (i, 0, 0, 0)),
            full(delta),
        ],
        out_specs=pl.BlockSpec((1, 3, ri, LANES), lambda i: (i, 0, 0, 0)),
        scratch_shapes=[
            pltpu.VMEM((LANES, LANES), jnp.bfloat16),
            pltpu.VMEM((3 * ri, LANES), jnp.bfloat16),
            pltpu.VMEM((3 * ri, LANES), jnp.float32),
        ],
        compiler_params=pltpu.CompilerParams(vmem_limit_bytes=VMEM_LIMIT),
        cost_estimate=pl.CostEstimate(
            flops=flops, bytes_accessed=4 * rows.size * 2, transcendentals=0
        ),
    )(rows, rows, rows, mask, kron_v, occ_cols, delta)


def response_kernel(first, second, weight, out):
    ri = first.shape[2]

    @pl.when(pl.program_id(0) == 0)
    def _():
        out[...] = jnp.zeros_like(out)

    for half, left in enumerate((first, second)):
        total = None
        for b in range(3):
            term = lax.dot_general(
                left[0, b],
                weight[0, b],
                (((1,), (1,)), ((), ())),
                preferred_element_type=jnp.float32,
            )
            total = term if total is None else total + term
        out[half] += total


def responses(first, second, weight, start):
    atoms, _, ri, _ = first.shape
    spec = lambda shift: pl.BlockSpec((1, 3, ri, LANES), lambda i, s=shift: (i + s, 0, 0, 0))
    return pl.pallas_call(
        response_kernel,
        grid=(atoms,),
        out_shape=jax.ShapeDtypeStruct((2, ri, ri), jnp.float32),
        in_specs=[spec(0), spec(0), spec(start)],
        out_specs=pl.BlockSpec((2, ri, ri), lambda i: (0, 0, 0)),
        compiler_params=pltpu.CompilerParams(vmem_limit_bytes=VMEM_LIMIT),
        cost_estimate=pl.CostEstimate(
            flops=atoms * 12 * ri * ri * LANES,
            bytes_accessed=atoms * 9 * ri * LANES * 2,
            transcendentals=0,
        ),
    )(first, second, weight)


def small_tables(occupied, virtual, atom_size, tensor_pattern, occupied_pattern, virtual_pattern, atoms):
    first = lax.axis_index("wide") * atoms
    total = atom_size.shape[0]

    def near(array, margin):
        pads = ((margin, margin),) + ((0, 0),) * (array.ndim - 1)
        return lax.dynamic_slice_in_dim(jnp.pad(array, pads), first, atoms + 2 * margin, 0)

    def partners(margin):
        own = first - margin + jnp.arange(atoms + 2 * margin)
        other = own[:, None] + jnp.arange(-1, 2)[None, :]
        return ((own >= 0) & (own < total))[:, None] & (other >= 0) & (other < total)

    sizes = near(atom_size, 2)
    count = atoms + 2
    flags = (near(tensor_pattern, 1) != 0) & partners(1)
    partner = jnp.stack([sizes[d : d + count] for d in range(3)], 1)
    lane = jnp.arange(LANES, dtype=jnp.int32)
    row_ok = (lane // BO)[None, None, :] < sizes[1 : 1 + count, None, None]
    column_ok = (lane % BO)[None, None, :] < partner[:, :, None]
    mask = (flags[:, :, None] & row_ok & column_ok).astype(jnp.bfloat16)

    occ_keep = ((near(occupied_pattern, 1) != 0) & partners(1)).astype(jnp.bfloat16)
    occ = near(occupied, 1) * occ_keep[:, :, None]
    occ = jnp.stack([occ[co : co + atoms, 2 - co] for co in range(3)], 1)
    occ = occ.reshape(atoms, 3, BO, BO)
    spread = (lane[None, :] // BO == jnp.arange(BO)[:, None]).astype(jnp.bfloat16)
    occ_cols = jnp.einsum(
        "acij,jl->acil", occ, spread, preferred_element_type=jnp.float32
    ).astype(jnp.bfloat16)
    delta = (lane[None, :] % BO == jnp.arange(BO)[:, None]).astype(jnp.bfloat16)

    vir_keep = ((near(virtual_pattern, 2) != 0) & partners(2)).astype(jnp.bfloat16)
    vir = (near(virtual, 2) * vir_keep[:, :, None]).reshape(atoms + 4, 3, BO, BO)
    short = jnp.arange(GROUP)
    same = (short[:, None] // BO == short[None, :] // BO).astype(jnp.bfloat16)
    kron_v = jnp.tile(vir, (1, 1, GROUP // BO, GROUP // BO)) * same
    return mask, occ_cols, delta, kron_v


def body(tensor, occupied, virtual, atom_size, tensor_pattern, occupied_pattern, virtual_pattern):
    wide = lax.axis_size("wide")
    narrow = lax.axis_size("narrow")
    atoms, _, ri, _ = tensor.shape
    me = lax.axis_index("narrow")
    up = [(i, i + 1) for i in range(wide - 1)]
    down = [(i + 1, i) for i in range(wide - 1)]
    sibling = [(i, i ^ 1) for i in range(narrow)]
    before = lax.ppermute(tensor[atoms - 1 :], "wide", up)
    after = lax.ppermute(tensor[:1], "wide", down)
    near = lax.ppermute(tensor, "narrow", sibling)
    far = []
    for step in range(2, narrow, 2):
        pairs = [(i, (i + step) % narrow) for i in range(narrow)]
        for a in range(atoms):
            direct = lax.ppermute(tensor[a : a + 1], "narrow", pairs)
            passed = lax.ppermute(direct, "narrow", sibling)
            far.append((step, a, direct, passed))

    mask, occ_cols, delta, kron_v = small_tables(
        occupied, virtual, atom_size, tensor_pattern, occupied_pattern, virtual_pattern, atoms
    )
    rows = jnp.concatenate([before, tensor, after], 0)
    weight = weights(rows, mask, kron_v, occ_cols, delta)
    parts = {0: responses(tensor, near, weight, 0)}
    for step, a, direct, passed in far:
        part = responses(direct, passed, weight, a)
        parts[step] = parts[step] + part if step in parts else part

    core = me % 2
    ordered = []
    for pair in range(narrow // 2):
        step = (me // 2 - pair) % (narrow // 2) * 2
        block = parts[0]
        for s in range(2, narrow, 2):
            block = jnp.where(step == s, parts[s], block)
        ordered.append(jnp.where(core == 0, block, block[::-1]))
    partial = jnp.concatenate(ordered, 0).reshape(wide, narrow * ri // wide, ri)
    shares = lax.all_to_all(partial.astype(jnp.bfloat16), "wide", 0, 0, tiled=True)
    return jnp.sum(shares.astype(jnp.float32), 0)


def solution(mesh):
    placed = (P("wide", None, "narrow", None), P(), P(), P(), P(), P(), P())
    return jax.shard_map(
        body, mesh=mesh, in_specs=placed, out_specs=P("wide", "narrow"), check_vma=False
    )
```

time: 562 us -> 246 us (0.44); the launches traced: 553 us -> 246 us
  waiting for transfers between devices: 214 us -> 96.6 us
  local copies, waits for them, and re-layouts: 138 us -> 35.9 us
  matrix products: 95.1 us -> 1.22 us
  Pallas kernels: 0 us -> 61.6 us
  blocking collectives: 75.2 us -> 20.1 us
  between operations: 14.1 us -> 0.27 us
  other arithmetic: 9.27 us -> 17.8 us
    reduce_scatter x2 -> x0, waiting for transfers between devices: 214 us -> none  [the longest x1 146 us: body(): lax.psum_scatter(partial_response, 'narrow', scatter_dimension=1, tiled=T...]
    ppermute x2 -> x11, waiting for transfers between devices: 0.01 us -> 96.6 us  [the longest x1 58.8 us: body(): before = lax.ppermute(tensor[atoms - 1:], 'wide', up)]
    dot_general x19 -> x1, matrix products: 95.1 us -> 1.22 us  [small_tables(): jnp.einsum('acij,jl->acil', occ, spread, preferred_element_type=jnp.float32)]
    pallas_call x0 -> x6, Pallas kernels: none -> 61.6 us  [the longest x1 35.6 us: weights(): pl.pallas_call(weight_kernel, grid=(atoms,), out_shape=jax.ShapeDtypeStru...]
    all_to_all x1, blocking collectives: 75.2 us -> 20.1 us  [body(): lax.all_to_all(partial.astype(jnp.bfloat16), 'wide', 0, 0, tiled=True)]
    concatenate x4 -> x0, local copies, waits for them, and re-layouts: 37.9 us -> none  [with_halo(): array = jnp.concatenate([before, array, after], axis=dim)]
    ppermute x2 -> x0, local copies, waits for them, and re-layouts: 17.6 us -> none  [the longest x1 8.94 us: with_halo(): before = lax.ppermute(last, axis, up)]
    another operation x12 -> x5, local copies, waits for them, and re-layouts: 40.3 us -> 23.2 us  [the longest x4 23.1 us: small_tables(): kron_v = jnp.tile(vir, (1, 1, GROUP // BO, GROUP // BO)) * same]
  transfers between devices with their start and end apart: 4 -> 11, of which waited for: 2 -> 3; matrix products, arithmetic and copies ran while one was open for 9% -> 17% of each run, Pallas kernels for 0% -> 21%
where the time goes in v1:
time: 246 us
  waiting for transfers between devices  96.6 us (39%)
  Pallas kernels  61.6 us (25%)
  local copies, waits for them, and re-layouts  35.9 us (15%)
  blocking collectives  20.1 us (8%)
  other arithmetic  17.8 us (7%)
  starting transfers between devices  12.2 us (5%)
    ppermute x1, waiting for transfers between devices, body(): before = lax.ppermute(tensor[atoms - 1:], 'wide', up)  58.8 us
    ppermute x4, waiting for transfers between devices, body(): direct = lax.ppermute(tensor[a:a + 1], 'narrow', pairs)  37.8 us
    pallas_call x1, Pallas kernels, weights(): pl.pallas_call(weight_kernel, grid=(atoms,), out_shape=jax.ShapeDtypeStru...  35.6 us
    pallas_call x5, Pallas kernels, responses(): pl.pallas_call(response_kernel, grid=(atoms,), out_shape=jax.ShapeDtypeSt...  26 us
    another operation x4, local copies, waits for them, and re-layouts, small_tables(): kron_v = jnp.tile(vir, (1, 1, GROUP // BO, GROUP // BO)) * same  23.1 us
    all_to_all x1, blocking collectives, body(): lax.all_to_all(partial.astype(jnp.bfloat16), 'wide', 0, 0, tiled=True)  20.1 us
    concatenate x1, other arithmetic, body(): rows = jnp.concatenate([before, tensor, after], 0)  7.02 us
    slice x1, local copies, waits for them, and re-layouts, body(): direct = lax.ppermute(tensor[a:a + 1], 'narrow', pairs)  5.69 us
  transfers between devices with their start and end apart: 11, of which 3 were waited for; matrix products, arithmetic and copies ran while one was open for 17% of the time, Pallas kernels for 21%

profile of v1, /device:TPU:0, one launch (start us, length us, event | category | flops | bytes accessed | tf_op | source)
XLA Modules:
  0.0 245.7 jit_solution(5097490971032557373)
XLA Ops:
  0.0 5.7 %fusion.25 = (bf16[1,3,256,1024]{3,2,1,0:T(8,128)(2,1)}, bf16[1,3,256,1024]{3,2,1,0:T(8,128)(2,1)}, bf16[1,3,256,1024]{3,2,1,0:T(8,128)(2,1)}, bf16[1,3,256,1024]{3,2,1,0:T(8,128)(2,1)}) fusion(bf16[4,3,256,1024]{3,2,1,0:T(8,128)(2,1)} %first.1), kind=kLoop, calls=%fused_computation.67 | loop fusion | bytes 12582912 | tf_op jit(solution)/shard_map/slice | solution.py:173
  5.7 1.3 collective-permute-start.3
  7.0 3.0 %collective-permute-start = (bf16[1,3,256,1024]{3,2,1,0:T(8,128)(2,1)}, bf16[1,3,256,1024]{3,2,1,0:T(8,128)(2,1)}, u32[]{:S(2)}, u32[]{:S(2)}) collective-permute-start(bf16[1,3,256,1024]{3,2,1,0:T(8,128)(2,1)} %get-tuple-element.10), channel_id=1, source_target_pairs={{0,2},{1,3},{2,0},{3,1},{4,6},{5,7},{6,4},{7,5},{8,10},{9,11},{10,... | collective-permute-start | bytes 4718600 | tf_op jit(solution)/shard_map/ppermute | solution.py:173
  10.0 4.6 %collective-permute-start.2 = (bf16[1,3,256,1024]{3,2,1,0:T(8,128)(2,1)}, bf16[1,3,256,1024]{3,2,1,0:T(8,128)(2,1)S(1)}, u32[]{:S(2)}, u32[]{:S(2)}) collective-permute-start(bf16[1,3,256,1024]{3,2,1,0:T(8,128)(2,1)} %get-tuple-element.9), channel_id=1, source_target_pairs={{0,4},{4,8},{8,12},{12,16},{16,20},{20,24},{24,28},{1,5},{5,9},{9,... | collective-permute-start | bytes 4718600 | tf_op jit(solution)/shard_map/ppermute | solution.py:166
  17.3 1.4 fusion.24
  20.3 58.8 %collective-permute-done.2 = bf16[1,3,256,1024]{3,2,1,0:T(8,128)(2,1)S(1)} collective-permute-done((bf16[1,3,256,1024]{3,2,1,0:T(8,128)(2,1)}, bf16[1,3,256,1024]{3,2,1,0:T(8,128)(2,1)S(1)}, u32[]{:S(2)}, u32[]{:S(2)}) %collective-permute-start.2) | collective-permute-done | bytes 1572896 | tf_op jit(solution)/shard_map/ppermute | solution.py:166
  79.1 1.5 collective-permute-start.4
  84.3 7.7 %tile.11 = bf16[8,3,8,32,8,32]{5,4,3,2,1,0:T(8,128)(2,1)} broadcast(bf16[8,3,32,32]{3,2,1,0:T(8,128)(2,1)S(1)} %copy.14), dimensions={0,1,3,5} | broadcast | bytes 3194880 | tf_op jit(solution)/shard_map/tile | solution.py:154
  92.0 14.4 %tile.12 = bf16[8,3,256,256]{3,2,1,0:T(8,128)(2,1)S(1)} reshape(bf16[8,3,8,32,8,32]{5,4,3,2,1,0:T(8,128)(2,1)} %tile.11) | data formatting | bytes 6291456 | tf_op jit(solution)/shard_map/tile | solution.py:154
  108.0 1.2 convolution_convert_fusion.occ_cols
  109.2 1.9 broadcast_multiply_fusion.kron_v
  111.2 5.5 %collective-permute-done.4.first = bf16[1,3,256,1024]{3,2,1,0:T(8,128)(2,1)} collective-permute-done((bf16[1,3,256,1024]{3,2,1,0:T(8,128)(2,1)}, bf16[1,3,256,1024]{3,2,1,0:T(8,128)(2,1)}, u32[]{:S(2)}, u32[]{:S(2)}) %collective-permute-start.4) | collective-permute-done | bytes 1572896 | tf_op jit(solution)/shard_map/ppermute | solution.py:173
  117.2 32.3 %collective-permute-done.6.first = bf16[1,3,256,1024]{3,2,1,0:T(8,128)(2,1)} collective-permute-done((bf16[1,3,256,1024]{3,2,1,0:T(8,128)(2,1)}, bf16[1,3,256,1024]{3,2,1,0:T(8,128)(2,1)}, u32[]{:S(2)}, u32[]{:S(2)}) %collective-permute-start.6) | collective-permute-done | bytes 1572896 | tf_op jit(solution)/shard_map/ppermute | solution.py:173
  150.0 7.0 %pad_maximum_fusion.before.here.after = bf16[6,3,256,1024]{3,2,1,0:T(8,128)(2,1)} fusion(bf16[1,3,256,1024]{3,2,1,0:T(8,128)(2,1)S(1)} %copy-done.6, bf16[4,3,256,1024]{3,2,1,0:T(8,128)(2,1)} %first.1, bf16[1,3,256,1024]{3,2,1,0:T(8,128)(2,1)S(1)} %copy-done.8), kind=kLoop, calls=%fused_computation | loop fusion | flops 9437184 | bytes 18874368 | tf_op jit(solution)/shard_map/concatenate | solution.py:180
  157.0 35.6 %shard_map.73.weight = bf16[4,3,256,1024]{3,2,1,0:T(8,128)(2,1)} custom-call(bf16[6,3,256,1024]{3,2,1,0:T(8,128)(2,1)} %pad_maximum_fusion.before.here.after, bf16[6,3,256,1024]{3,2,1,0:T(8,128)(2,1)} %pad_maximum_fusion.before.here.after, bf16[6,3,256,1024]{3,2,1,0:T(8,128)(2,1)} %pad_maximum_fusion.before.here.after, ...), custom_call_target="tpu_custom_call" | custom-call | flops 29527900160 | bytes 37748736 | tf_op jit(solution)/shard_map/pallas_call | solution.py:54
  193.8 4.2 %shard_map.75 = f32[2,256,256]{2,1,0:T(8,128)} custom-call(bf16[1,3,256,1024]{3,2,1,0:T(8,128)(2,1)} %collective-permute-done.4.first, bf16[1,3,256,1024]{3,2,1,0:T(8,128)(2,1)} %copy-done.9, bf16[4,3,256,1024]{3,2,1,0:T(8,128)(2,1)} %shard_map.73.weight), custom_call_target="tpu_custom_call" | custom-call | flops 805306368 | bytes 4718592 | tf_op jit(solution)/shard_map/pallas_call | solution.py:103
  198.0 1.2 copy-done.10
  199.2 4.2 %shard_map.74 = f32[2,256,256]{2,1,0:T(8,128)} custom-call(bf16[1,3,256,1024]{3,2,1,0:T(8,128)(2,1)} %collective-permute-done.first, bf16[1,3,256,1024]{3,2,1,0:T(8,128)(2,1)} %copy-done.10, bf16[4,3,256,1024]{3,2,1,0:T(8,128)(2,1)} %shard_map.73.weight), custom_call_target="tpu_custom_call" | custom-call | flops 805306368 | bytes 4718592 | tf_op jit(solution)/shard_map/pallas_call | solution.py:103
  204.5 4.2 %shard_map.76 = f32[2,256,256]{2,1,0:T(8,128)} custom-call(bf16[1,3,256,1024]{3,2,1,0:T(8,128)(2,1)} %collective-permute-done.6.first, bf16[1,3,256,1024]{3,2,1,0:T(8,128)(2,1)} %copy-done.11, bf16[4,3,256,1024]{3,2,1,0:T(8,128)(2,1)} %shard_map.73.weight), custom_call_target="tpu_custom_call" | custom-call | flops 805306368 | bytes 4718592 | tf_op jit(solution)/shard_map/pallas_call | solution.py:103
  208.7 1.2 copy-done.12
  209.8 4.2 %shard_map.77 = f32[2,256,256]{2,1,0:T(8,128)} custom-call(bf16[1,3,256,1024]{3,2,1,0:T(8,128)(2,1)} %collective-permute-done.8.first, bf16[1,3,256,1024]{3,2,1,0:T(8,128)(2,1)} %copy-done.12, bf16[4,3,256,1024]{3,2,1,0:T(8,128)(2,1)} %shard_map.73.weight), custom_call_target="tpu_custom_call" | custom-call | flops 805306368 | bytes 4718592 | tf_op jit(solution)/shard_map/pallas_call | solution.py:103
  214.0 9.3 %shard_map.78 = f32[2,256,256]{2,1,0:T(8,128)} custom-call(bf16[4,3,256,1024]{3,2,1,0:T(8,128)(2,1)} %first.1, bf16[4,3,256,1024]{3,2,1,0:T(8,128)(2,1)} %collective-permute-done.10.second, bf16[4,3,256,1024]{3,2,1,0:T(8,128)(2,1)} %shard_map.73.weight), custom_call_target="tpu_custom_call" | custom-call | flops 3221225472 | bytes 18874368 | tf_op jit(solution)/shard_map/pallas_call | solution.py:103
  223.4 1.3 broadcast_select_fusion.1
  224.9 20.1 %all_to_all.5 = bf16[8,128,256]{2,1,0:T(8,128)(2,1)S(1)} all-to-all(bf16[8,128,256]{2,1,0:T(8,128)(2,1)S(1)} %bitcast.18), channel_id=1, replica_groups=mesh['wide'=8,'narrow'=4] {'wide'}, dimensions={0} | all-to-all | bytes 1048576 | tf_op jit(solution)/shard_map/all_to_all | solution.py:196
  (80 shorter events, 13.7 us)
Async XLA Ops:
  0.0 16.5 %copy-start.18 = (s32[32]{0:T(128)S(1)}, s32[32]{0:T(128)}, u32[]{:S(2)}) copy-start(s32[32]{0:T(128)} %param.10) | copy-start | bytes 388
  0.0 18.6 %copy-start.14 = (bf16[32,3,1024]{2,0,1:T(8,128)(2,1)S(1)}, bf16[32,3,1024]{2,0,1:T(8,128)(2,1)}, u32[]{:S(2)}) copy-start(bf16[32,3,1024]{2,0,1:T(8,128)(2,1)} %param.8) | copy-start | bytes 589828
  0.0 19.5 %copy-start.15 = (bf16[32,3,1024]{2,0,1:T(8,128)(2,1)S(1)}, bf16[32,3,1024]{2,0,1:T(8,128)(2,1)}, u32[]{:S(2)}) copy-start(bf16[32,3,1024]{2,0,1:T(8,128)(2,1)} %param.9) | copy-start | bytes 589828
  5.7 74.9 %collective-permute-start.3 = (bf16[1,3,256,1024]{3,2,1,0:T(8,128)(2,1)}, bf16[1,3,256,1024]{3,2,1,0:T(8,128)(2,1)S(1)}, u32[]{:S(2)}, u32[]{:S(2)}) collective-permute-start(bf16[1,3,256,1024]{3,2,1,0:T(8,128)(2,1)} %get-tuple-element.10), channel_id=1, source_target_pairs={{4,0},{8,4},{12,8},{16,12},{20,16},{24,20},{28,24},{5,1},{9,5},{13... | collective-permute-start | bytes 4718600 | tf_op jit(solution)/shard_map/ppermute | solution.py:167
  7.0 109.7 %collective-permute-start = (bf16[1,3,256,1024]{3,2,1,0:T(8,128)(2,1)}, bf16[1,3,256,1024]{3,2,1,0:T(8,128)(2,1)}, u32[]{:S(2)}, u32[]{:S(2)}) collective-permute-start(bf16[1,3,256,1024]{3,2,1,0:T(8,128)(2,1)} %get-tuple-element.10), channel_id=1, source_target_pairs={{0,2},{1,3},{2,0},{3,1},{4,6},{5,7},{6,4},{7,5},{8,10},{9,11},{10,... | collective-permute-start | bytes 4718600 | tf_op jit(solution)/shard_map/ppermute | solution.py:173
  10.0 69.1 %collective-permute-start.2 = (bf16[1,3,256,1024]{3,2,1,0:T(8,128)(2,1)}, bf16[1,3,256,1024]{3,2,1,0:T(8,128)(2,1)S(1)}, u32[]{:S(2)}, u32[]{:S(2)}) collective-permute-start(bf16[1,3,256,1024]{3,2,1,0:T(8,128)(2,1)} %get-tuple-element.9), channel_id=1, source_target_pairs={{0,4},{4,8},{8,12},{12,16},{16,20},{20,24},{24,28},{1,5},{5,9},{9,... | collective-permute-start | bytes 4718600 | tf_op jit(solution)/shard_map/ppermute | solution.py:166
  14.7 134.8 %collective-permute-start.8 = (bf16[1,3,256,1024]{3,2,1,0:T(8,128)(2,1)}, bf16[1,3,256,1024]{3,2,1,0:T(8,128)(2,1)}, u32[]{:S(2)}, u32[]{:S(2)}) collective-permute-start(bf16[1,3,256,1024]{3,2,1,0:T(8,128)(2,1)} %get-tuple-element.9), channel_id=1, source_target_pairs={{0,2},{1,3},{2,0},{3,1},{4,6},{5,7},{6,4},{7,5},{8,10},{9,11},{10,... | collective-permute-start | bytes 4718600 | tf_op jit(solution)/shard_map/ppermute | solution.py:173
  14.8 199.3 %collective-permute-start.10 = (bf16[4,3,256,1024]{3,2,1,0:T(8,128)(2,1)}, bf16[4,3,256,1024]{3,2,1,0:T(8,128)(2,1)}, u32[]{:S(2)}, u32[]{:S(2)}) collective-permute-start(bf16[4,3,256,1024]{3,2,1,0:T(8,128)(2,1)} %first.1), channel_id=1, source_target_pairs={{0,1},{1,0},{2,3},{3,2},{4,5},{5,4},{6,7},{7,6},{8,9},{9,8},{10,11... | collective-permute-start | bytes 18874376 | tf_op jit(solution)/shard_map/ppermute | solution.py:168
  79.1 5.2 %copy-start.7 = (bf16[1,3,256,1024]{3,2,1,0:T(8,128)(2,1)}, bf16[1,3,256,1024]{3,2,1,0:T(8,128)(2,1)S(1)}, u32[]{:S(2)}) copy-start(bf16[1,3,256,1024]{3,2,1,0:T(8,128)(2,1)S(1)} %collective-permute-done.2) | copy-start | bytes 4718596
  79.1 37.6 %collective-permute-start.4 = (bf16[1,3,256,1024]{3,2,1,0:T(8,128)(2,1)}, bf16[1,3,256,1024]{3,2,1,0:T(8,128)(2,1)}, u32[]{:S(2)}, u32[]{:S(2)}) collective-permute-start(bf16[1,3,256,1024]{3,2,1,0:T(8,128)(2,1)} %get-tuple-element.7), channel_id=1, source_target_pairs={{0,2},{1,3},{2,0},{3,1},{4,6},{5,7},{6,4},{7,5},{8,10},{9,11},{10,... | collective-permute-start | bytes 4718600 | tf_op jit(solution)/shard_map/ppermute | solution.py:173
  80.6 68.8 %collective-permute-start.6 = (bf16[1,3,256,1024]{3,2,1,0:T(8,128)(2,1)}, bf16[1,3,256,1024]{3,2,1,0:T(8,128)(2,1)}, u32[]{:S(2)}, u32[]{:S(2)}) collective-permute-start(bf16[1,3,256,1024]{3,2,1,0:T(8,128)(2,1)} %get-tuple-element.8), channel_id=1, source_target_pairs={{0,2},{1,3},{2,0},{3,1},{4,6},{5,7},{6,4},{7,5},{8,10},{9,11},{10,... | collective-permute-start | bytes 4718600 | tf_op jit(solution)/shard_map/ppermute | solution.py:173
  92.0 14.5 %copy-start.17 = (s32[6]{0:T(128)S(1)}, s32[6]{0:T(128)}, u32[]{:S(2)}) copy-start(s32[6]{0:T(128)} %get-tuple-element.16) | copy-start | bytes 76
  92.0 15.9 %copy-start.16 = (s32[256]{0:T(256)S(1)}, s32[256]{0:T(256)}, u32[]{:S(2)}) copy-start(s32[256]{0:T(256)} %and_select_fusion) | copy-start | bytes 3076
  92.0 16.0 %copy-start.13 = (bf16[4,3,32,32]{3,2,0,1:T(8,128)(2,1)S(1)}, bf16[4,3,32,32]{3,2,0,1:T(8,128)(2,1)}, u32[]{:S(2)}) copy-start(bf16[4,3,32,32]{3,2,0,1:T(8,128)(2,1)} %reshape.240) | copy-start | bytes 73732
  109.2 40.7 %copy-start.6 = (bf16[1,3,256,1024]{3,2,1,0:T(8,128)(2,1)S(1)}, bf16[1,3,256,1024]{3,2,1,0:T(8,128)(2,1)}, u32[]{:S(2)}) copy-start(bf16[1,3,256,1024]{3,2,1,0:T(8,128)(2,1)} %copy-done.5) | copy-start | bytes 4718596
  109.2 40.7 %copy-start.8 = (bf16[1,3,256,1024]{3,2,1,0:T(8,128)(2,1)S(1)}, bf16[1,3,256,1024]{3,2,1,0:T(8,128)(2,1)}, u32[]{:S(2)}) copy-start(bf16[1,3,256,1024]{3,2,1,0:T(8,128)(2,1)} %copy-done.7) | copy-start | bytes 4718596
  116.7 76.0 %collective-permute-start.5 = (bf16[1,3,256,1024]{3,2,1,0:T(8,128)(2,1)}, bf16[1,3,256,1024]{3,2,1,0:T(8,128)(2,1)S(1)}, u32[]{:S(2)}, u32[]{:S(2)}) collective-permute-start(bf16[1,3,256,1024]{3,2,1,0:T(8,128)(2,1)} %collective-permute-done.4.first), channel_id=1, source_target_pairs={{0,1},{1,0},{2,3},{3,2},{4,5},{5,4},{6,7},{7,6},{8,9},{9,8},{10,11... | collective-permute-start | bytes 4718600 | tf_op jit(solution)/shard_map/ppermute | solution.py:174
  116.7 81.3 %collective-permute-start.1 = (bf16[1,3,256,1024]{3,2,1,0:T(8,128)(2,1)}, bf16[1,3,256,1024]{3,2,1,0:T(8,128)(2,1)S(1)}, u32[]{:S(2)}, u32[]{:S(2)}) collective-permute-start(bf16[1,3,256,1024]{3,2,1,0:T(8,128)(2,1)} %collective-permute-done.first), channel_id=1, source_target_pairs={{0,1},{1,0},{2,3},{3,2},{4,5},{5,4},{6,7},{7,6},{8,9},{9,8},{10,11... | collective-permute-start | bytes 4718600 | tf_op jit(solution)/shard_map/ppermute | solution.py:174
  149.4 53.9 %collective-permute-start.7 = (bf16[1,3,256,1024]{3,2,1,0:T(8,128)(2,1)}, bf16[1,3,256,1024]{3,2,1,0:T(8,128)(2,1)S(1)}, u32[]{:S(2)}, u32[]{:S(2)}) collective-permute-start(bf16[1,3,256,1024]{3,2,1,0:T(8,128)(2,1)} %collective-permute-done.6.first), channel_id=1, source_target_pairs={{0,1},{1,0},{2,3},{3,2},{4,5},{5,4},{6,7},{7,6},{8,9},{9,8},{10,11... | collective-permute-start | bytes 4718600 | tf_op jit(solution)/shard_map/ppermute | solution.py:174
  149.4 59.2 %collective-permute-start.9 = (bf16[1,3,256,1024]{3,2,1,0:T(8,128)(2,1)}, bf16[1,3,256,1024]{3,2,1,0:T(8,128)(2,1)S(1)}, u32[]{:S(2)}, u32[]{:S(2)}) collective-permute-start(bf16[1,3,256,1024]{3,2,1,0:T(8,128)(2,1)} %collective-permute-done.8.first), channel_id=1, source_target_pairs={{0,1},{1,0},{2,3},{3,2},{4,5},{5,4},{6,7},{7,6},{8,9},{9,8},{10,11... | collective-permute-start | bytes 4718600 | tf_op jit(solution)/shard_map/ppermute | solution.py:174
  214.0 9.3 %copy-start.1 = (f32[2,256,256]{2,1,0:T(8,128)S(1)}, f32[2,256,256]{2,1,0:T(8,128)}, u32[]{:S(2)}) copy-start(f32[2,256,256]{2,1,0:T(8,128)} %shard_map.75) | copy-start | bytes 1572868
  214.0 9.3 %copy-start.2 = (f32[2,256,256]{2,1,0:T(8,128)S(1)}, f32[2,256,256]{2,1,0:T(8,128)}, u32[]{:S(2)}) copy-start(f32[2,256,256]{2,1,0:T(8,128)} %shard_map.74) | copy-start | bytes 1572868
  214.0 9.3 %copy-start.3 = (f32[2,256,256]{2,1,0:T(8,128)S(1)}, f32[2,256,256]{2,1,0:T(8,128)}, u32[]{:S(2)}) copy-start(f32[2,256,256]{2,1,0:T(8,128)} %shard_map.76) | copy-start | bytes 1572868
  214.0 9.3 %copy-start.4 = (f32[2,256,256]{2,1,0:T(8,128)S(1)}, f32[2,256,256]{2,1,0:T(8,128)}, u32[]{:S(2)}) copy-start(f32[2,256,256]{2,1,0:T(8,128)} %shard_map.77) | copy-start | bytes 1572868
  (6 other events, 9.7 us)
